TPU v7x, 32 devices: a whole 2x2x4 slice. The times are simulated.
32 devices in a mesh: cases: 2 (over x), row: 8 (over z, y), col: 2 (over core).
Axes of the slice: x: 2, y: 2, z: 4, core: 2. Of those that a mesh axis runs over, the one named last changes fastest.
Arguments:
- markov_head: bfloat16 [32, 500, 500], P(('cases', 'row')), parts along dimension 0, may hold values from -0.0625 to 0.0625
- markov_tail: bfloat16 [32, 500, 500], P(('cases', 'col')), parts along dimension 0, may hold values from -0.0625 to 0.0625
- probes: bfloat16 [16000, 128], P(('cases', 'col')), parts along dimension 0, may hold values from -6 to 6
Outputs:
- sketch: float32 [16000, 128], P(('cases', 'row')), parts along dimension 0
- back_now: float32 [16000, 128], P(('cases', 'col')), parts along dimension 0
- back_next: float32 [16000, 128], P(('cases', 'col')), parts along dimension 0
There are 2 independent parts, one for each index of `cases`. A program takes and returns all parts, laid end to end along the dimension named above; each array names one. Nothing has to cross between parts.
All inputs are finite; a program needn't handle non-finite values.
Results may differ from a plain program's by a relative error of at most 0.0022.
Values may be sent and summed in bfloat16 or wider, within the bound.
A program may use at most 128 MiB of HBM per device.

v0:
```python
import jax
import jax.numpy as jnp
from jax import lax
from jax.sharding import PartitionSpec as P


def spread(x, axis, root):
    mine = lax.axis_index(axis) == root
    return lax.psum(jnp.where(mine, x, jnp.zeros_like(x)), axis)


def from_behind(x, axis, by):
    peers = lax.axis_size(axis)
    pairs = [(i, i + by) for i in range(peers) if 0 <= i + by < peers]
    return lax.ppermute(x, axis, pairs)


def store_slot(window, target, shard):
    slot_count = window.shape[0]
    inside = (target >= 0) & (target < slot_count)
    placed = jnp.clip(target, 0, slot_count - 1)
    present = lax.dynamic_index_in_dim(window, placed, 0, keepdims=False)
    return lax.dynamic_update_index_in_dim(window, jnp.where(inside, shard, present), placed, 0)


def body(markov_head, markov_tail, probes):
    rows_held = markov_head.shape[0]
    order = markov_head.shape[1]
    cols_held = markov_tail.shape[0]
    columns = probes.shape[1]
    row_count = lax.axis_size("row")
    row_place = lax.axis_index("row")
    col_place = lax.axis_index("col")
    strides = cols_held // rows_held
    slot_count = strides + 1
    blocks = probes.reshape(cols_held, order, columns)
    leading = spread(markov_tail, "col", 0)
    full_tail = jnp.concatenate([leading, markov_tail], axis=0)
    window = jnp.zeros((slot_count, rows_held, order, order), markov_head.dtype)

    def march_turn(number, status):
        window_now, carried = status
        window_now = store_slot(window_now, number - col_place * strides, carried)
        carried = from_behind(carried, "row", -1)
        return (window_now, carried)

    window, carried = lax.fori_loop(0, 2 * strides, march_turn, (window, markov_head))
    window = store_slot(window, 2 * strides - col_place * strides, carried)
    shard_ids = row_place + col_place * strides + jnp.arange(slot_count, dtype=jnp.int32)
    offsets = jnp.clip((shard_ids - row_count) * rows_held, 0, 2 * cols_held - rows_held)

    def tail_piece(anchor):
        return lax.dynamic_slice_in_dim(full_tail, anchor, rows_held, 0)

    from_tail = jax.vmap(tail_piece)(offsets)
    window = jnp.where((shard_ids >= row_count)[:, None, None, None], from_tail, window)
    window = window.reshape(slot_count * rows_held, order, order)
    partial_rows = jnp.stack(
        [
            jnp.einsum(
                "jpq,jqk->pk",
                window[offset : offset + cols_held],
                blocks,
                preferred_element_type=jnp.float32,
            )
            for offset in range(rows_held)
        ]
    ).reshape(rows_held * order, columns)
    sketch = lax.psum(partial_rows, "col")
    rounded = sketch.astype(jnp.bfloat16).reshape(rows_held, order, columns)
    current_sum = jnp.zeros((cols_held, order, columns), jnp.float32)
    shifted_sum = jnp.zeros((cols_held, order, columns), jnp.float32)
    for offset in range(rows_held):
        current_sum = current_sum + jnp.einsum(
            "jqp,qk->jpk",
            window[offset : offset + cols_held],
            rounded[offset],
            preferred_element_type=jnp.float32,
        )
        shifted_sum = shifted_sum + jnp.einsum(
            "jqp,qk->jpk",
            window[offset + 1 : offset + 1 + cols_held],
            rounded[offset],
            preferred_element_type=jnp.float32,
        )
    back_now, back_next = lax.psum(
        (
            current_sum.reshape(cols_held * order, columns),
            shifted_sum.reshape(cols_held * order, columns),
        ),
        "row",
    )
    return (sketch, back_now, back_next)


def solution(mesh):
    placed = (
        P(("cases", "row"), None, None),
        P(("cases", "col"), None, None),
        P(("cases", "col"), None),
    )
    return jax.shard_map(
        body,
        mesh=mesh,
        in_specs=placed,
        out_specs=(P(("cases", "row"), None), P(("cases", "col"), None), P(("cases", "col"), None)),
        check_vma=False,
    )
```

profile of v0, /device:TPU:1, one launch (start us, length us, event | category | flops | bytes accessed | tf_op | source)
XLA Modules:
  0.0 459.1 jit_solution(12658244585146072324)
XLA Ops:
  7.2 8.1 %broadcast_select_fusion.2 = (bf16[8,500,500]{2,1,0:T(8,128)(2,1)}, bf16[8,500,500]{2,1,0:T(8,128)(2,1)}) fusion(pred[]{:T(512)S(6)} %eq.3, bf16[8,500,500]{2,0,1:T(8,128)(2,1)} %param.6), kind=kLoop, calls=%fused_computation.7 | loop fusion | flops 2000000 | bytes 12000001 | tf_op jit(solution)/shard_map/jit(_where)/select_n | solution.py:9
  15.4 4.9 %broadcast_in_dim.31 = bf16[5,2,500,500]{3,1,2,0:T(2,128)(2,1)} broadcast(bf16[]{:T(256)} %constant.77.clone.1), dimensions={} | broadcast | bytes 5000002 | tf_op jit(solution)/shard_map/broadcast_in_dim | solution.py:39
  20.3 190.7 %while.17 = (s32[]{:T(128)}, bf16[5,2,500,500]{3,1,2,0:T(2,128)(2,1)}, bf16[2,500,500]{2,0,1:T(2,128)(2,1)S(1)}, s32[]{:T(128)}, s32[]{:T(128)}, /*index=5*/s32[]{:T(128)}, s32[]{:T(128)}, s32[]{:T(128)}) while((s32[]{:T(128)}, bf16[5,2,500,500]{3,1,2,0:T(2,128)(2,1)}, bf16[2,500,500]{2,0,1:T(2,128)(2,1)S(1)}, s32[]{:T(128)}, s32[]{:T(128)}, ...), condition=%wide.region_2.3_spmd, body=%wide.region_1.2_spmd.sunk | while | flops 500008 | bytes 11024191 | solution.py:47
  24.2 2.1 fusion.17
  26.3 21.0 %collective-permute-done = bf16[2,500,500]{2,0,1:T(2,128)(2,1)S(1)} collective-permute-done((bf16[2,500,500]{2,0,1:T(2,128)(2,1)S(1)}, bf16[2,500,500]{2,0,1:T(2,128)(2,1)S(1)}, u32[]{:S(2)}, u32[]{:S(2)}) %collective-permute-start) | collective-permute-done | bytes 1000032 | tf_op jit(solution)/shard_map/while/body/eval_jaxpr/ppermute | solution.py:15
  53.3 20.0 %collective-permute-done = bf16[2,500,500]{2,0,1:T(2,128)(2,1)S(1)} collective-permute-done((bf16[2,500,500]{2,0,1:T(2,128)(2,1)S(1)}, bf16[2,500,500]{2,0,1:T(2,128)(2,1)S(1)}, u32[]{:S(2)}, u32[]{:S(2)}) %collective-permute-start) | collective-permute-done | bytes 1000032 | tf_op jit(solution)/shard_map/while/body/eval_jaxpr/ppermute | solution.py:15
  79.4 19.1 %collective-permute-done = bf16[2,500,500]{2,0,1:T(2,128)(2,1)S(1)} collective-permute-done((bf16[2,500,500]{2,0,1:T(2,128)(2,1)S(1)}, bf16[2,500,500]{2,0,1:T(2,128)(2,1)S(1)}, u32[]{:S(2)}, u32[]{:S(2)}) %collective-permute-start) | collective-permute-done | bytes 1000032 | tf_op jit(solution)/shard_map/while/body/eval_jaxpr/ppermute | solution.py:15
  104.5 18.2 %collective-permute-done = bf16[2,500,500]{2,0,1:T(2,128)(2,1)S(1)} collective-permute-done((bf16[2,500,500]{2,0,1:T(2,128)(2,1)S(1)}, bf16[2,500,500]{2,0,1:T(2,128)(2,1)S(1)}, u32[]{:S(2)}, u32[]{:S(2)}) %collective-permute-start) | collective-permute-done | bytes 1000032 | tf_op jit(solution)/shard_map/while/body/eval_jaxpr/ppermute | solution.py:15
  128.8 17.3 %collective-permute-done = bf16[2,500,500]{2,0,1:T(2,128)(2,1)S(1)} collective-permute-done((bf16[2,500,500]{2,0,1:T(2,128)(2,1)S(1)}, bf16[2,500,500]{2,0,1:T(2,128)(2,1)S(1)}, u32[]{:S(2)}, u32[]{:S(2)}) %collective-permute-start) | collective-permute-done | bytes 1000032 | tf_op jit(solution)/shard_map/while/body/eval_jaxpr/ppermute | solution.py:15
  152.1 16.4 %collective-permute-done = bf16[2,500,500]{2,0,1:T(2,128)(2,1)S(1)} collective-permute-done((bf16[2,500,500]{2,0,1:T(2,128)(2,1)S(1)}, bf16[2,500,500]{2,0,1:T(2,128)(2,1)S(1)}, u32[]{:S(2)}, u32[]{:S(2)}) %collective-permute-start) | collective-permute-done | bytes 1000032 | tf_op jit(solution)/shard_map/while/body/eval_jaxpr/ppermute | solution.py:15
  174.5 15.5 %collective-permute-done = bf16[2,500,500]{2,0,1:T(2,128)(2,1)S(1)} collective-permute-done((bf16[2,500,500]{2,0,1:T(2,128)(2,1)S(1)}, bf16[2,500,500]{2,0,1:T(2,128)(2,1)S(1)}, u32[]{:S(2)}, u32[]{:S(2)}) %collective-permute-start) | collective-permute-done | bytes 1000032 | tf_op jit(solution)/shard_map/while/body/eval_jaxpr/ppermute | solution.py:15
  195.9 15.1 %collective-permute-done = bf16[2,500,500]{2,0,1:T(2,128)(2,1)S(1)} collective-permute-done((bf16[2,500,500]{2,0,1:T(2,128)(2,1)S(1)}, bf16[2,500,500]{2,0,1:T(2,128)(2,1)S(1)}, u32[]{:S(2)}, u32[]{:S(2)}) %collective-permute-start) | collective-permute-done | bytes 1000032 | tf_op jit(solution)/shard_map/while/body/eval_jaxpr/ppermute | solution.py:15
  211.0 5.7 %copy.24 = bf16[5,2,500,500]{3,2,1,0:T(8,128)(2,1)} copy(bf16[5,2,500,500]{3,1,2,0:T(2,128)(2,1)} %get-tuple-element.111) | data formatting | bytes 10000000 | tf_op jit(solution)/shard_map/while | solution.py:47
  220.2 7.5 %pad_maximum_fusion = bf16[16,500,500]{2,1,0:T(8,128)(2,1)} fusion(bf16[8,500,500]{2,1,0:T(8,128)(2,1)} %get-tuple-element.134, bf16[8,500,500]{2,1,0:T(8,128)(2,1)} %all-reduce.6.cloned.1.call-done), kind=kLoop, calls=%fused_computation.5 | loop fusion | flops 4000000 | bytes 16000000 | tf_op jit(solution)/shard_map/concatenate | solution.py:38
  227.7 7.0 %gather_fusion = bf16[5,2,500,500]{3,2,1,0:T(8,128)(2,1)} fusion(bf16[16,500,500]{2,1,0:T(8,128)(2,1)} %pad_maximum_fusion, s32[5]{0:T(128)S(1)} %fusion.6), kind=kCustom, calls=%fused_computation | custom fusion | bytes 10000060 | tf_op jit(solution)/shard_map/vmap()/gather | solution.py:53
  234.7 4.6 %broadcast_select_fusion.1 = bf16[5,2,500,500]{3,2,1,0:T(8,128)(2,1)S(1)} fusion(bf16[5,2,500,500]{3,2,1,0:T(8,128)(2,1)} %gather_fusion, bf16[5,2,500,500]{3,2,1,0:T(8,128)(2,1)} %bitcast_dynamic-update-slice_fusion, pred[5]{0:T(512)(128)(4,1)S(1)} %add_compare_fusion), kind=kLoop, calls=%fused_computation.6 | loop fusion | flops 2500000 | bytes 15000005 | tf_op jit(solution)/shard_map/jit(_where)/select_n | solution.py:56
  239.3 2.5 fusion.7
  247.0 27.4 %all-reduce.8.cloned.1.call-done = f32[1000,128]{1,0:T(8,128)} async-done(((f32[1000,128]{1,0:T(8,128)}), f32[1000,128]{1,0:T(8,128)}) %all-reduce.8.cloned.1.call-update) | async-done | bytes 512016 | tf_op jit(solution)/shard_map/psum | solution.py:69
  275.4 3.5 fusion.2
  278.9 3.5 convolution_add_fusion.1
  283.8 3.5 fusion.3
  287.3 3.5 convolution_add_fusion
  292.3 155.2 %all-reduce.10.cloned.1.call-done = (f32[4000,128]{1,0:T(8,128)}, f32[4000,128]{1,0:T(8,128)}) async-done(((f32[4000,128]{1,0:T(8,128)}, f32[4000,128]{1,0:T(8,128)}), (f32[4000,128]{1,0:T(8,128)}, f32[4000,128]{1,0:T(8,128)})) %all-reduce.10.cloned.1.call-update) | async-done | bytes 4096016 | tf_op jit(solution)/shard_map/psum | solution.py:86
  448.2 3.0 copy.54
  (64 shorter events, 60.3 us)
Async XLA Ops:
  7.2 213.0 %all-reduce.6.cloned.1.call-start = ((), (), s32[]{:S(2)}) async-start(), calls=%async_computation | async-start | bytes 8257536 | tf_op jit(solution)/shard_map/psum | solution.py:9
  15.3 5.0 %copy-start.1 = (bf16[2,500,500]{2,0,1:T(2,128)(2,1)S(1)}, bf16[2,500,500]{2,0,1:T(2,128)(2,1)}, u32[]{:S(2)}) copy-start(bf16[2,500,500]{2,0,1:T(2,128)(2,1)} %param.5) | copy-start | bytes 3000004
  15.3 259.0 %all-reduce.8.cloned.1.call-start = ((), (), s32[]{:S(2)}) async-start(), calls=%async_computation.1 | async-start | bytes 1024000 | tf_op jit(solution)/shard_map/psum | solution.py:69
  21.0 26.3 %collective-permute-start = (bf16[2,500,500]{2,0,1:T(2,128)(2,1)S(1)}, bf16[2,500,500]{2,0,1:T(2,128)(2,1)S(1)}, u32[]{:S(2)}, u32[]{:S(2)}) collective-permute-start(bf16[2,500,500]{2,0,1:T(2,128)(2,1)S(1)} %copy.43), channel_id=1, source_target_pairs={{2,0},{4,2},{6,4},{8,6},{10,8},{12,10},{14,12},{3,1},{5,3},{7,5},{... | collective-permute-start | bytes 3000008 | tf_op jit(solution)/shard_map/while/body/eval_jaxpr/ppermute | solution.py:15
  48.0 25.3 %collective-permute-start = (bf16[2,500,500]{2,0,1:T(2,128)(2,1)S(1)}, bf16[2,500,500]{2,0,1:T(2,128)(2,1)S(1)}, u32[]{:S(2)}, u32[]{:S(2)}) collective-permute-start(bf16[2,500,500]{2,0,1:T(2,128)(2,1)S(1)} %copy.43), channel_id=1, source_target_pairs={{2,0},{4,2},{6,4},{8,6},{10,8},{12,10},{14,12},{3,1},{5,3},{7,5},{... | collective-permute-start | bytes 3000008 | tf_op jit(solution)/shard_map/while/body/eval_jaxpr/ppermute | solution.py:15
  74.1 24.4 %collective-permute-start = (bf16[2,500,500]{2,0,1:T(2,128)(2,1)S(1)}, bf16[2,500,500]{2,0,1:T(2,128)(2,1)S(1)}, u32[]{:S(2)}, u32[]{:S(2)}) collective-permute-start(bf16[2,500,500]{2,0,1:T(2,128)(2,1)S(1)} %copy.43), channel_id=1, source_target_pairs={{2,0},{4,2},{6,4},{8,6},{10,8},{12,10},{14,12},{3,1},{5,3},{7,5},{... | collective-permute-start | bytes 3000008 | tf_op jit(solution)/shard_map/while/body/eval_jaxpr/ppermute | solution.py:15
  99.2 23.5 %collective-permute-start = (bf16[2,500,500]{2,0,1:T(2,128)(2,1)S(1)}, bf16[2,500,500]{2,0,1:T(2,128)(2,1)S(1)}, u32[]{:S(2)}, u32[]{:S(2)}) collective-permute-start(bf16[2,500,500]{2,0,1:T(2,128)(2,1)S(1)} %copy.43), channel_id=1, source_target_pairs={{2,0},{4,2},{6,4},{8,6},{10,8},{12,10},{14,12},{3,1},{5,3},{7,5},{... | collective-permute-start | bytes 3000008 | tf_op jit(solution)/shard_map/while/body/eval_jaxpr/ppermute | solution.py:15
  123.5 22.6 %collective-permute-start = (bf16[2,500,500]{2,0,1:T(2,128)(2,1)S(1)}, bf16[2,500,500]{2,0,1:T(2,128)(2,1)S(1)}, u32[]{:S(2)}, u32[]{:S(2)}) collective-permute-start(bf16[2,500,500]{2,0,1:T(2,128)(2,1)S(1)} %copy.43), channel_id=1, source_target_pairs={{2,0},{4,2},{6,4},{8,6},{10,8},{12,10},{14,12},{3,1},{5,3},{7,5},{... | collective-permute-start | bytes 3000008 | tf_op jit(solution)/shard_map/while/body/eval_jaxpr/ppermute | solution.py:15
  146.8 21.7 %collective-permute-start = (bf16[2,500,500]{2,0,1:T(2,128)(2,1)S(1)}, bf16[2,500,500]{2,0,1:T(2,128)(2,1)S(1)}, u32[]{:S(2)}, u32[]{:S(2)}) collective-permute-start(bf16[2,500,500]{2,0,1:T(2,128)(2,1)S(1)} %copy.43), channel_id=1, source_target_pairs={{2,0},{4,2},{6,4},{8,6},{10,8},{12,10},{14,12},{3,1},{5,3},{7,5},{... | collective-permute-start | bytes 3000008 | tf_op jit(solution)/shard_map/while/body/eval_jaxpr/ppermute | solution.py:15
  169.2 20.8 %collective-permute-start = (bf16[2,500,500]{2,0,1:T(2,128)(2,1)S(1)}, bf16[2,500,500]{2,0,1:T(2,128)(2,1)S(1)}, u32[]{:S(2)}, u32[]{:S(2)}) collective-permute-start(bf16[2,500,500]{2,0,1:T(2,128)(2,1)S(1)} %copy.43), channel_id=1, source_target_pairs={{2,0},{4,2},{6,4},{8,6},{10,8},{12,10},{14,12},{3,1},{5,3},{7,5},{... | collective-permute-start | bytes 3000008 | tf_op jit(solution)/shard_map/while/body/eval_jaxpr/ppermute | solution.py:15
  190.7 20.4 %collective-permute-start = (bf16[2,500,500]{2,0,1:T(2,128)(2,1)S(1)}, bf16[2,500,500]{2,0,1:T(2,128)(2,1)S(1)}, u32[]{:S(2)}, u32[]{:S(2)}) collective-permute-start(bf16[2,500,500]{2,0,1:T(2,128)(2,1)S(1)} %copy.43), channel_id=1, source_target_pairs={{2,0},{4,2},{6,4},{8,6},{10,8},{12,10},{14,12},{3,1},{5,3},{7,5},{... | collective-permute-start | bytes 3000008 | tf_op jit(solution)/shard_map/while/body/eval_jaxpr/ppermute | solution.py:15
  211.0 5.7 %copy-start.5 = (bf16[4000,128]{1,0:T(8,128)(2,1)S(1)}, bf16[4000,128]{1,0:T(8,128)(2,1)}, u32[]{:S(2)}) copy-start(bf16[4000,128]{1,0:T(8,128)(2,1)} %param.7) | copy-start | bytes 3072004
  239.3 3.7 copy-start
  241.8 3.9 copy-start.2
  246.7 200.7 %all-reduce.10.cloned.1.call-start = ((), (), s32[]{:S(2)}) async-start(), calls=%async_computation.2 | async-start | bytes 8192000 | tf_op jit(solution)/shard_map/psum | solution.py:86
  290.8 156.6 %copy-start.4 = (f32[1000,128]{1,0:T(8,128)S(1)}, f32[1000,128]{1,0:T(8,128)}, u32[]{:S(2)}) copy-start(f32[1000,128]{1,0:T(8,128)} %all-reduce.8.cloned.1.call-done) | copy-start | bytes 1536004
  447.4 3.8 copy-start.3
Sparse Core Ops, SparseCore 0:
  15.4 30.8 all-reduce.5
  246.8 27.4 all-reduce.7
  292.4 154.9 all-reduce.9
where the time goes:
time: 461 us; the launch traced here: 459 us
  waiting for transfers between devices  325 us (70%)
  local copies, waits for them, and re-layouts  53.4 us (12%)
  other arithmetic  39 us (8%)
  matrix products  16.6 us (4%)
  between operations  13.9 us (3%)
  starting transfers between devices  10.7 us (2%)
    psum x1, waiting for transfers between devices, body(): lax.psum((current_sum.reshape(cols_held * order, columns), shifted_sum.re...  155 us
    ppermute x8, waiting for transfers between devices, from_behind(): return lax.ppermute(x, axis, pairs)  143 us
    psum x1, waiting for transfers between devices, body(): sketch = lax.psum(partial_rows, 'col')  27.4 us
    dynamic_update_slice x9, other arithmetic, store_slot(): lax.dynamic_update_index_in_dim(window, jnp.where(inside, shard, present)...  17.7 us
    dynamic_slice x9, local copies, waits for them, and re-layouts, store_slot(): present = lax.dynamic_index_in_dim(window, placed, 0, keepdims=False)  17.3 us
    ppermute x8, starting transfers between devices, from_behind(): return lax.ppermute(x, axis, pairs)  10.3 us
  transfers between devices with their start and end apart: 11, of which 10 were waited for; matrix products, arithmetic and copies ran while one was open for 11% of the time, Pallas kernels for 0%

commit v1 on v0

--- a/solution.py
+++ b/solution.py
@@ -1,7 +1,12 @@
 import jax
 import jax.numpy as jnp
 from jax import lax
+from jax.experimental import pallas as pl
+from jax.experimental.pallas import tpu as pltpu
 from jax.sharding import PartitionSpec as P
+
+LANES = 128
+MESH = pl.DeviceIdType.MESH
 
 
 def spread(x, axis, root):
@@ -93,14 +98,327 @@
     return (sketch, back_now, back_next)
 
 
+def gathered_kernel(head_ref, tail_ref, probe_ref, sk_ref, y_ref, m, px, st, acc, yacc,
+                    local_sem, zsend, ysend, ssend, piece_recv, sib_recv, xsend, xrecv):
+    f32 = jnp.float32
+    r = lax.axis_index("row")
+    c = lax.axis_index("col")
+    other = 1 - c
+    z, y = r // 2, r % 2
+    mate = r + 1 - 2 * y
+    layers = lax.axis_size("row") // 2
+
+    load_head = pltpu.make_async_copy(head_ref, m.at[pl.ds(2 * r, 2)], local_sem.at[0])
+    load_probe = pltpu.make_async_copy(
+        probe_ref, px.at[:, pl.ds(pl.multiple_of((9 - 8 * c) * LANES, LANES), 8 * LANES)], local_sem.at[1])
+    load_tail = pltpu.make_async_copy(tail_ref, m.at[pl.ds(16 + 8 * c, 8)], local_sem.at[2])
+    load_head.start()
+    load_probe.start()
+    load_tail.start()
+
+    barrier = pltpu.get_barrier_semaphore()
+
+    def greet(row, col):
+        pl.semaphore_signal(barrier, inc=1, device_id={"row": row, "col": col}, device_id_type=MESH)
+
+    greet(r, other)
+    greet(mate, c)
+
+    @pl.when(z > 0)
+    def _():
+        greet(r - 2, c)
+
+    @pl.when(z < layers - 1)
+    def _():
+        greet(r + 2, c)
+
+    zero_columns = jnp.zeros((px.shape[0], LANES), px.dtype)
+    px[:, 0:LANES] = zero_columns
+    px[:, 17 * LANES:18 * LANES] = zero_columns
+    zero_rows = jnp.zeros((LANES, st.shape[1]), st.dtype)
+    st[0:LANES, :] = zero_rows
+    st[17 * LANES:18 * LANES, :] = zero_rows
+    acc[...] = jnp.zeros_like(acc)
+    pl.semaphore_wait(barrier, 2 + (z > 0).astype(jnp.int32) + (z < layers - 1).astype(jnp.int32))
+
+    def along_z(s, up):
+        return pltpu.make_async_remote_copy(
+            m.at[2 * s + c], m.at[2 * s + c], zsend.at[up * 8 + s], piece_recv.at[s],
+            device_id={"row": r + 4 * up - 2, "col": c}, device_id_type=MESH)
+
+    def along_y(s):
+        return pltpu.make_async_remote_copy(
+            m.at[2 * s + c], m.at[2 * s + c], ysend.at[s], piece_recv.at[s],
+            device_id={"row": mate, "col": c}, device_id_type=MESH)
+
+    def to_core(s):
+        return pltpu.make_async_remote_copy(
+            m.at[2 * s + c], m.at[2 * s + c], ssend.at[s], sib_recv.at[s],
+            device_id={"row": r, "col": other}, device_id_type=MESH)
+
+    def from_core(s):
+        return pltpu.make_async_remote_copy(
+            m.at[2 * s + other], m.at[2 * s + other], ssend.at[s], sib_recv.at[s],
+            device_id={"row": r, "col": other}, device_id_type=MESH)
+
+    def swap(ref_of, slot):
+        return pltpu.make_async_remote_copy(
+            ref_of(c), ref_of(c), xsend.at[slot], xrecv.at[slot],
+            device_id={"row": r, "col": other}, device_id_type=MESH)
+
+    def swapped(ref_of, slot):
+        return pltpu.make_async_remote_copy(
+            ref_of(other), ref_of(other), xsend.at[slot], xrecv.at[slot],
+            device_id={"row": r, "col": other}, device_id_type=MESH)
+
+    def probe_part(core):
+        return px.at[:, pl.ds(pl.multiple_of((9 - 8 * core) * LANES, LANES), 8 * LANES)]
+
+    def tail_part(core):
+        return m.at[pl.ds(16 + 8 * core, 8)]
+
+    def sketch_part(core):
+        return st.at[pl.ds(pl.multiple_of((9 - 8 * core) * LANES, LANES), 8 * LANES), :]
+
+    load_head.wait()
+    along_y(r).start()
+
+    @pl.when(z > 0)
+    def _():
+        along_z(r, 0).start()
+
+    @pl.when(z < layers - 1)
+    def _():
+        along_z(r, 1).start()
+
+    load_probe.wait()
+    swap(probe_part, 0).start()
+    load_tail.wait()
+
+    @pl.when(c == 0)
+    def _():
+        swap(tail_part, 1).start()
+
+    def use(first, count):
+        def turn(step, carry):
+            k = first + step // 4
+            g = step % 4
+            lag = k - 8 * c - 2 * g
+
+            @pl.when((lag >= 0) & (lag <= 16))
+            def _():
+                spot = pl.multiple_of((16 - lag) * LANES, LANES)
+                acc[g] += jnp.dot(m[k], px[:, pl.ds(spot, 2 * LANES)], preferred_element_type=f32)
+
+            return carry
+
+        lax.fori_loop(0, 4 * count, turn, 0)
+
+    def wanted(s, core):
+        return (core == 0) | (s >= 4)
+
+    def use_chip(s):
+        @pl.when(wanted(s, c))
+        def _():
+            from_core(s).wait_recv()
+            use(2 * s, 2)
+
+    def each_side(base, distance, act):
+        for up in (0, 1):
+            there = z + distance * (2 * up - 1)
+            s = base + 2 * distance * (2 * up - 1)
+
+            @pl.when((there >= 0) & (there < layers))
+            def _(s=s, up=up):
+                act(s, up)
+
+    def take_z(s, up):
+        along_y(s).wait_recv()
+        onward = (z < layers - 1) if up == 0 else (z > 0)
+
+        @pl.when(onward)
+        def _():
+            along_z(s, 1 - up).start()
+
+        along_y(s).start()
+
+        @pl.when(wanted(s, other))
+        def _():
+            to_core(s).start()
+
+    def take_y(s, up=0):
+        along_y(s).wait_recv()
+
+        @pl.when(wanted(s, other))
+        def _():
+            to_core(s).start()
+
+    swapped(probe_part, 0).wait_recv()
+    use(16 + 8 * c, 7)
+
+    each_side(r, 1, take_z)
+    take_y(mate)
+
+    @pl.when(wanted(r, c))
+    def _():
+        use(2 * r, 2)
+
+    @pl.when(c == 1)
+    def _():
+        swapped(tail_part, 1).wait_recv()
+        use(16, 4)
+
+    each_side(r, 2, take_z)
+    each_side(mate, 1, take_y)
+
+    @pl.when(c == 1)
+    def _():
+        use(20, 4)
+
+    use_chip(mate)
+    each_side(r, 1, lambda s, up: use_chip(s))
+    each_side(r, 3, take_z)
+    each_side(mate, 2, take_y)
+    each_side(r, 2, lambda s, up: use_chip(s))
+    each_side(mate, 1, lambda s, up: use_chip(s))
+    each_side(mate, 3, take_y)
+    each_side(r, 3, lambda s, up: use_chip(s))
+    each_side(mate, 2, lambda s, up: use_chip(s))
+    each_side(mate, 3, lambda s, up: use_chip(s))
+
+    for g in range(4):
+        flipped = acc[g].T.astype(st.dtype)
+        for half in range(2):
+            spot = pl.multiple_of((16 - 8 * c - 2 * g - half) * LANES, LANES)
+            st[pl.ds(spot, LANES), :] = flipped[half * LANES:(half + 1) * LANES]
+    swap(sketch_part, 2).start()
+    mine = (r // 4) == c
+
+    def row_copy():
+        return pltpu.make_async_remote_copy(
+            acc.at[r % 4], acc.at[4], xsend.at[3], xrecv.at[3],
+            device_id={"row": r, "col": other}, device_id_type=MESH)
+
+    @pl.when(mine)
+    def _():
+        row_copy().start()
+        sk_ref[0] = acc[r % 4, :, 0:LANES]
+        sk_ref[1] = acc[r % 4, :, LANES:2 * LANES]
+
+    swapped(sketch_part, 2).wait_recv()
+
+    def back_pair(g, carry):
+        def add(lag, carry):
+            k = 8 * c + jnp.minimum(2 * g + lag, 23)
+            spot = pl.multiple_of((16 - lag) * LANES, LANES)
+            yacc[...] += jnp.dot(st[pl.ds(spot, 2 * LANES), :], m[k], preferred_element_type=f32)
+            return carry
+
+        yacc[...] = jnp.zeros_like(yacc)
+        lax.fori_loop(0, 17, add, 0)
+        upright = yacc[...].T
+        y_ref[2 * g] = upright[:, 0:LANES]
+        y_ref[2 * g + 1] = upright[:, LANES:2 * LANES]
+        return carry
+
+    lax.fori_loop(0, 5, back_pair, 0)
+
+    @pl.when(jnp.logical_not(mine))
+    def _():
+        row_copy().wait_recv()
+        sk_ref[0] = acc[4, :, 0:LANES]
+        sk_ref[1] = acc[4, :, LANES:2 * LANES]
+
+    @pl.when(mine)
+    def _():
+        row_copy().wait_send()
+
+    def sent(s, up):
+        onward = (z < layers - 1) if up == 0 else (z > 0)
+
+        @pl.when(onward)
+        def _():
+            along_z(s, 1 - up).wait_send()
+
+        along_y(s).wait_send()
+
+        @pl.when(wanted(s, other))
+        def _():
+            to_core(s).wait_send()
+
+    def sent_core(s, up=0):
+        @pl.when(wanted(s, other))
+        def _():
+            to_core(s).wait_send()
+
+    along_y(r).wait_send()
+
+    @pl.when(z > 0)
+    def _():
+        along_z(r, 0).wait_send()
+
+    @pl.when(z < layers - 1)
+    def _():
+        along_z(r, 1).wait_send()
+
+    sent_core(mate)
+    for distance in (1, 2, 3):
+        each_side(r, distance, sent)
+        each_side(mate, distance, sent_core)
+    swap(probe_part, 0).wait_send()
+
+    @pl.when(c == 0)
+    def _():
+        swap(tail_part, 1).wait_send()
+
+    swap(sketch_part, 2).wait_send()
+
+
+def gathered_body(markov_head, markov_tail, probes):
+    order = markov_head.shape[1]
+    columns = probes.shape[1]
+    blocks = probes.reshape(8, order, columns)[::-1]
+    wide = blocks.transpose(1, 0, 2).reshape(order, 8 * columns)
+    anywhere = pl.BlockSpec(memory_space=pl.ANY)
+    near = pl.BlockSpec(memory_space=pltpu.VMEM)
+    dma = pltpu.SemaphoreType.DMA
+    sketch, back = pl.pallas_call(
+        gathered_kernel,
+        out_shape=(jax.ShapeDtypeStruct((2, order, columns), jnp.float32),
+                   jax.ShapeDtypeStruct((10, order, columns), jnp.float32)),
+        in_specs=[anywhere] * 3,
+        out_specs=(near, near),
+        scratch_shapes=[
+            pltpu.VMEM((32, order, order), jnp.bfloat16),
+            pltpu.VMEM((order, 18 * columns), jnp.bfloat16),
+            pltpu.VMEM((18 * columns, order), jnp.bfloat16),
+            pltpu.VMEM((5, order, 2 * columns), jnp.float32),
+            pltpu.VMEM((2 * columns, order), jnp.float32),
+            dma((3,)), dma((16,)), dma((8,)), dma((8,)), dma((8,)), dma((8,)), dma((4,)), dma((4,)),
+        ],
+        compiler_params=pltpu.CompilerParams(
+            collective_id=0, has_side_effects=True, vmem_limit_bytes=56 * 1024 * 1024),
+    )(markov_head, markov_tail, wide)
+    return (sketch.reshape(2 * order, columns),
+            back[0:8].reshape(8 * order, columns),
+            back[1:9].reshape(8 * order, columns))
+
+
 def solution(mesh):
     placed = (
         P(("cases", "row"), None, None),
         P(("cases", "col"), None, None),
         P(("cases", "col"), None),
     )
+    fits = mesh.shape["row"] == 8 and mesh.shape["col"] == 2
+
+    def parts(markov_head, markov_tail, probes):
+        shapes = (markov_head.shape[0], markov_tail.shape[0], probes.shape[1])
+        chosen = gathered_body if fits and shapes == (2, 8, LANES) else body
+        return chosen(markov_head, markov_tail, probes)
+
     return jax.shard_map(
-        body,
+        parts,
         mesh=mesh,
         in_specs=placed,
         out_specs=(P(("cases", "row"), None), P(("cases", "col"), None), P(("cases", "col"), None)),

time: 461 us -> 111 us (0.24)
  waiting for transfers between devices: 325 us -> 0 us
  Pallas kernels: 0 us -> 91.7 us
  other arithmetic: 39 us -> 0 us
  local copies, waits for them, and re-layouts: 53.4 us -> 18.6 us
  matrix products: 16.6 us -> 0 us
  between operations: 13.9 us -> 0.68 us
  starting transfers between devices: 10.7 us -> 0 us
    psum x3 -> x0, waiting for transfers between devices: 183 us -> none  [the longest x1 155 us: body(): lax.psum((current_sum.reshape(cols_held * order, columns), shifted_sum.re...]
    ppermute x8 -> x0, waiting for transfers between devices: 143 us -> none  [from_behind(): return lax.ppermute(x, axis, pairs)]
    pallas_call x0 -> x1, Pallas kernels: none -> 91.7 us  [gathered_body(): pl.pallas_call(gathered_kernel, out_shape=(jax.ShapeDtypeStruct((2, order...]
    dynamic_update_slice x9 -> x0, other arithmetic: 17.7 us -> none  [store_slot(): lax.dynamic_update_index_in_dim(window, jnp.where(inside, shard, present)...]
    dynamic_slice x9 -> x0, local copies, waits for them, and re-layouts: 17.3 us -> none  [store_slot(): present = lax.dynamic_index_in_dim(window, placed, 0, keepdims=False)]
    dot_general x6 -> x0, matrix products: 16.6 us -> none  [the longest x2 6.98 us: body(): jnp.einsum('jqp,qk->jpk', window[offset:offset + cols_held], rounded[offs...]
    select_n x2 -> x0, other arithmetic: 12.7 us -> none  [the longest x1 8.05 us: spread(): return lax.psum(jnp.where(mine, x, jnp.zeros_like(x)), axis)]
    ppermute x8 -> x0, starting transfers between devices: 10.3 us -> none  [from_behind(): return lax.ppermute(x, axis, pairs)]
  transfers between devices with their start and end apart: 11 -> 0, of which waited for: 10 -> 0; matrix products, arithmetic and copies ran while one was open for 11% -> 0% of each run, Pallas kernels for 0% -> 0%
where the time goes in v1:
time: 111 us
  Pallas kernels  91.7 us (83%)
  local copies, waits for them, and re-layouts  18.6 us (17%)
    pallas_call x1, Pallas kernels, gathered_body(): pl.pallas_call(gathered_kernel, out_shape=(jax.ShapeDtypeStruct((2, order...  91.7 us
    unnamed x8, local copies, waits for them, and re-layouts  8.27 us
    slice x1, local copies, waits for them, and re-layouts, gathered_body(): back[1:9].reshape(8 * order, columns)  3.81 us
    reshape x1, local copies, waits for them, and re-layouts, gathered_body(): back[1:9].reshape(8 * order, columns)  2.8 us

profile of v1, /device:TPU:1, one launch (start us, length us, event | category | flops | bytes accessed | tf_op | source)
XLA Modules:
  0.0 110.9 jit_solution(17671030397694604214)
XLA Ops:
  0.6 0.0 copy-start.1
  0.6 2.4 %copy.10.head_ref = bf16[2,500,500]{2,1,0:T(8,128)(2,1)} copy(bf16[2,500,500]{2,0,1:T(2,128)(2,1)} %param.3) | data formatting | bytes 2000000 | tf_op args[0]
  3.1 0.0 copy-done.1
  3.1 0.2 reshape.21
  3.2 0.1 reverse_bitcast_fusion
  3.3 0.1 copy.9
  3.5 0.0 copy-start
  3.5 0.1 pad
  3.6 1.2 %copy.12 = bf16[63,8,8,128]{3,1,2,0:T(8,128)(2,1)} copy(bf16[63,8,8,128]{3,2,1,0:T(8,128)(2,1)S(1)} %bitcast.5) | data formatting | bytes 2064384
  4.8 1.2 %copy-done = bf16[8,500,500]{2,0,1:T(8,128)(2,1)S(1)} copy-done((bf16[8,500,500]{2,0,1:T(8,128)(2,1)S(1)}, bf16[8,500,500]{2,0,1:T(8,128)(2,1)}, u32[]{:S(2)}) %copy-start) | copy-done | bytes 4000024
  6.0 3.3 %copy.11.tail_ref = bf16[8,500,500]{2,1,0:T(8,128)(2,1)} copy(bf16[8,500,500]{2,0,1:T(8,128)(2,1)S(1)} %copy-done) | data formatting | bytes 8000000 | tf_op args[1]
  9.3 91.7 %shard_map.58 = (f32[2,500,128]{2,1,0:T(8,128)}, f32[10,500,128]{2,1,0:T(8,128)}) custom-call(bf16[2,500,500]{2,1,0:T(8,128)(2,1)} %copy.10.head_ref, bf16[8,500,500]{2,1,0:T(8,128)(2,1)} %copy.11.tail_ref, bf16[500,1024]{1,0:T(8,128)(2,1)} %bitcast.6), custom_call_target="tpu_custom_call" | custom-call | tf_op jit(solution)/shard_map/pallas_call | solution.py:385
  101.0 1.9 %reshape.23 = f32[1000,128]{1,0:T(8,128)} reshape(f32[2,500,128]{2,1,0:T(8,128)} %get-tuple-element.5) | data formatting | bytes 1024000 | tf_op jit(solution)/shard_map/reshape | solution.py:402
  102.9 3.8 %fusion = (f32[8,500,128]{2,1,0:T(8,128)}, f32[8,500,128]{2,1,0:T(8,128)S(1)}) fusion(f32[10,500,128]{2,1,0:T(8,128)} %get-tuple-element.6), kind=kLoop, calls=%fused_computation.1 | loop fusion | bytes 8192000 | tf_op jit(solution)/shard_map/slice | solution.py:404
  106.7 2.8 %reshape.25 = f32[4000,128]{1,0:T(8,128)} reshape(f32[8,500,128]{2,1,0:T(8,128)} %get-tuple-element.7) | data formatting | bytes 4096000 | tf_op jit(solution)/shard_map/reshape | solution.py:404
  109.5 1.4 %reshape.24 = f32[4000,128]{1,0:T(8,128)} reshape(f32[8,500,128]{2,1,0:T(8,128)S(1)} %get-tuple-element.8) | data formatting | bytes 4096000 | tf_op jit(solution)/shard_map/reshape | solution.py:403
Async XLA Ops:
  0.6 2.4 %copy-start.1 = (bf16[4000,128]{1,0:T(8,128)(2,1)S(1)}, bf16[4000,128]{1,0:T(8,128)(2,1)}, u32[]{:S(2)}) copy-start(bf16[4000,128]{1,0:T(8,128)(2,1)} %param.5) | copy-start | bytes 3072004
  3.5 2.5 %copy-start = (bf16[8,500,500]{2,0,1:T(8,128)(2,1)S(1)}, bf16[8,500,500]{2,0,1:T(8,128)(2,1)}, u32[]{:S(2)}) copy-start(bf16[8,500,500]{2,0,1:T(8,128)(2,1)} %param.4) | copy-start | bytes 12000004

commit v2 on v1

--- a/solution.py
+++ b/solution.py
@@ -7,6 +7,7 @@
 
 LANES = 128
 MESH = pl.DeviceIdType.MESH
+UNROLL = {4: 19, 5: 5}
 
 
 def spread(x, axis, root):
@@ -98,7 +99,7 @@
     return (sketch, back_now, back_next)
 
 
-def gathered_kernel(head_ref, tail_ref, probe_ref, sk_ref, y_ref, m, px, st, acc, yacc,
+def gathered_kernel(head_ref, tail_ref, probe_ref, sk_ref, now_ref, next_ref, m, px, st, acc, yacc,
                     local_sem, zsend, ysend, ssend, piece_recv, sib_recv, xsend, xrecv):
     f32 = jnp.float32
     r = lax.axis_index("row")
@@ -110,7 +111,7 @@
 
     load_head = pltpu.make_async_copy(head_ref, m.at[pl.ds(2 * r, 2)], local_sem.at[0])
     load_probe = pltpu.make_async_copy(
-        probe_ref, px.at[:, pl.ds(pl.multiple_of((9 - 8 * c) * LANES, LANES), 8 * LANES)], local_sem.at[1])
+        probe_ref, px.at[:, pl.ds(pl.multiple_of((12 - 8 * c) * LANES, LANES), 8 * LANES)], local_sem.at[1])
     load_tail = pltpu.make_async_copy(tail_ref, m.at[pl.ds(16 + 8 * c, 8)], local_sem.at[2])
     load_head.start()
     load_probe.start()
@@ -132,12 +133,12 @@
     def _():
         greet(r + 2, c)
 
-    zero_columns = jnp.zeros((px.shape[0], LANES), px.dtype)
-    px[:, 0:LANES] = zero_columns
-    px[:, 17 * LANES:18 * LANES] = zero_columns
-    zero_rows = jnp.zeros((LANES, st.shape[1]), st.dtype)
-    st[0:LANES, :] = zero_rows
-    st[17 * LANES:18 * LANES, :] = zero_rows
+    zero_columns = jnp.zeros((px.shape[0], 4 * LANES), px.dtype)
+    px[:, 0:4 * LANES] = zero_columns
+    px[:, 20 * LANES:24 * LANES] = zero_columns
+    zero_rows = jnp.zeros((4 * LANES, st.shape[1]), st.dtype)
+    st[0:4 * LANES, :] = zero_rows
+    st[20 * LANES:24 * LANES, :] = zero_rows
     acc[...] = jnp.zeros_like(acc)
     pl.semaphore_wait(barrier, 2 + (z > 0).astype(jnp.int32) + (z < layers - 1).astype(jnp.int32))
 
@@ -172,13 +173,13 @@
             device_id={"row": r, "col": other}, device_id_type=MESH)
 
     def probe_part(core):
-        return px.at[:, pl.ds(pl.multiple_of((9 - 8 * core) * LANES, LANES), 8 * LANES)]
+        return px.at[:, pl.ds(pl.multiple_of((12 - 8 * core) * LANES, LANES), 8 * LANES)]
 
     def tail_part(core):
         return m.at[pl.ds(16 + 8 * core, 8)]
 
     def sketch_part(core):
-        return st.at[pl.ds(pl.multiple_of((9 - 8 * core) * LANES, LANES), 8 * LANES), :]
+        return st.at[pl.ds(pl.multiple_of((12 - 8 * core) * LANES, LANES), 8 * LANES), :]
 
     load_head.wait()
     along_y(r).start()
@@ -207,7 +208,7 @@
 
             @pl.when((lag >= 0) & (lag <= 16))
             def _():
-                spot = pl.multiple_of((16 - lag) * LANES, LANES)
+                spot = pl.multiple_of((19 - lag) * LANES, LANES)
                 acc[g] += jnp.dot(m[k], px[:, pl.ds(spot, 2 * LANES)], preferred_element_type=f32)
 
             return carry
@@ -289,10 +290,11 @@
     for g in range(4):
         flipped = acc[g].T.astype(st.dtype)
         for half in range(2):
-            spot = pl.multiple_of((16 - 8 * c - 2 * g - half) * LANES, LANES)
+            spot = pl.multiple_of((19 - 8 * c - 2 * g - half) * LANES, LANES)
             st[pl.ds(spot, LANES), :] = flipped[half * LANES:(half + 1) * LANES]
     swap(sketch_part, 2).start()
     mine = (r // 4) == c
+    order = acc.shape[1]
 
     def row_copy():
         return pltpu.make_async_remote_copy(
@@ -302,32 +304,38 @@
     @pl.when(mine)
     def _():
         row_copy().start()
-        sk_ref[0] = acc[r % 4, :, 0:LANES]
-        sk_ref[1] = acc[r % 4, :, LANES:2 * LANES]
+        sk_ref[0:order] = acc[r % 4, :, 0:LANES]
+        sk_ref[order:2 * order] = acc[r % 4, :, LANES:2 * LANES]
 
     swapped(sketch_part, 2).wait_recv()
 
-    def back_pair(g, carry):
-        def add(lag, carry):
-            k = 8 * c + jnp.minimum(2 * g + lag, 23)
-            spot = pl.multiple_of((16 - lag) * LANES, LANES)
-            yacc[...] += jnp.dot(st[pl.ds(spot, 2 * LANES), :], m[k], preferred_element_type=f32)
+    for first, wide in ((0, 4), (4, 5)):
+        rows = wide * LANES
+
+        def add(turn, carry, first=first, wide=wide, rows=rows):
+            total = None
+            for part in range(UNROLL[wide]):
+                lag = UNROLL[wide] * turn + part
+                spot = pl.multiple_of((19 - lag) * LANES, LANES)
+                term = jnp.dot(st[pl.ds(spot, rows), :], m[8 * c + first + lag], preferred_element_type=f32)
+                total = term if total is None else total + term
+            yacc[0:rows] += total
             return carry
 
-        yacc[...] = jnp.zeros_like(yacc)
-        lax.fori_loop(0, 17, add, 0)
-        upright = yacc[...].T
-        y_ref[2 * g] = upright[:, 0:LANES]
-        y_ref[2 * g + 1] = upright[:, LANES:2 * LANES]
-        return carry
-
-    lax.fori_loop(0, 5, back_pair, 0)
+        yacc[0:rows] = jnp.zeros((rows, yacc.shape[1]), f32)
+        lax.fori_loop(0, (15 + wide) // UNROLL[wide], add, 0)
+        for block in range(first, first + wide):
+            upright = yacc[(block - first) * LANES:(block - first + 1) * LANES].T
+            if block < 8:
+                now_ref[block * order:(block + 1) * order] = upright
+            if block > 0:
+                next_ref[(block - 1) * order:block * order] = upright
 
     @pl.when(jnp.logical_not(mine))
     def _():
         row_copy().wait_recv()
-        sk_ref[0] = acc[4, :, 0:LANES]
-        sk_ref[1] = acc[4, :, LANES:2 * LANES]
+        sk_ref[0:order] = acc[4, :, 0:LANES]
+        sk_ref[order:2 * order] = acc[4, :, LANES:2 * LANES]
 
     @pl.when(mine)
     def _():
@@ -382,26 +390,24 @@
     anywhere = pl.BlockSpec(memory_space=pl.ANY)
     near = pl.BlockSpec(memory_space=pltpu.VMEM)
     dma = pltpu.SemaphoreType.DMA
-    sketch, back = pl.pallas_call(
+    return pl.pallas_call(
         gathered_kernel,
-        out_shape=(jax.ShapeDtypeStruct((2, order, columns), jnp.float32),
-                   jax.ShapeDtypeStruct((10, order, columns), jnp.float32)),
+        out_shape=(jax.ShapeDtypeStruct((2 * order, columns), jnp.float32),
+                   jax.ShapeDtypeStruct((8 * order, columns), jnp.float32),
+                   jax.ShapeDtypeStruct((8 * order, columns), jnp.float32)),
         in_specs=[anywhere] * 3,
-        out_specs=(near, near),
+        out_specs=(near, near, near),
         scratch_shapes=[
             pltpu.VMEM((32, order, order), jnp.bfloat16),
-            pltpu.VMEM((order, 18 * columns), jnp.bfloat16),
-            pltpu.VMEM((18 * columns, order), jnp.bfloat16),
+            pltpu.VMEM((order, 24 * columns), jnp.bfloat16),
+            pltpu.VMEM((24 * columns, order), jnp.bfloat16),
             pltpu.VMEM((5, order, 2 * columns), jnp.float32),
-            pltpu.VMEM((2 * columns, order), jnp.float32),
+            pltpu.VMEM((5 * columns, order), jnp.float32),
             dma((3,)), dma((16,)), dma((8,)), dma((8,)), dma((8,)), dma((8,)), dma((4,)), dma((4,)),
         ],
         compiler_params=pltpu.CompilerParams(
             collective_id=0, has_side_effects=True, vmem_limit_bytes=56 * 1024 * 1024),
     )(markov_head, markov_tail, wide)
-    return (sketch.reshape(2 * order, columns),
-            back[0:8].reshape(8 * order, columns),
-            back[1:9].reshape(8 * order, columns))
 
 
 def solution(mesh):

time: 111 us -> 94.7 us (0.85)
  Pallas kernels: 91.7 us -> 78.8 us
  local copies, waits for them, and re-layouts: 18.6 us -> 15 us
    pallas_call x1, Pallas kernels: 91.7 us -> 78.8 us  [gathered_body(): pl.pallas_call(gathered_kernel, out_shape=(jax.ShapeDtypeStruct((2 * orde...]
    unnamed x8 -> x13, local copies, waits for them, and re-layouts: 8.27 us -> 14.6 us
    reshape x3 -> x0, local copies, waits for them, and re-layouts: 6.09 us -> none  [the longest x1 2.8 us: gathered_body(): back[1:9].reshape(8 * order, columns)]
    slice x1 -> x0, local copies, waits for them, and re-layouts: 3.81 us -> none  [gathered_body(): back[1:9].reshape(8 * order, columns)]
where the time goes in v2:
time: 94.7 us; the launch traced here: 94.5 us
  Pallas kernels  78.8 us (83%)
  local copies, waits for them, and re-layouts  15 us (16%)
    pallas_call x1, Pallas kernels, gathered_body(): pl.pallas_call(gathered_kernel, out_shape=(jax.ShapeDtypeStruct((2 * orde...  78.8 us
    unnamed x13, local copies, waits for them, and re-layouts  14.6 us

profile of v2, /device:TPU:1, one launch (start us, length us, event | category | flops | bytes accessed | tf_op | source)
XLA Modules:
  0.0 94.5 jit_solution(1827729787295153341)
XLA Ops:
  0.6 0.0 copy-start.2
  0.6 2.4 %copy.10.head_ref = bf16[2,500,500]{2,1,0:T(8,128)(2,1)} copy(bf16[2,500,500]{2,0,1:T(2,128)(2,1)} %param.3) | data formatting | bytes 2000000 | tf_op args[0]
  3.1 0.0 copy-done.2
  3.1 0.2 reshape.12
  3.2 0.1 reverse_bitcast_fusion
  3.3 0.1 copy.9
  3.5 0.0 copy-start
  3.5 0.1 pad
  3.6 1.2 %copy.12 = bf16[63,8,8,128]{3,1,2,0:T(8,128)(2,1)} copy(bf16[63,8,8,128]{3,2,1,0:T(8,128)(2,1)S(1)} %bitcast.5) | data formatting | bytes 2064384
  4.8 1.2 %copy-done = bf16[8,500,500]{2,0,1:T(8,128)(2,1)S(1)} copy-done((bf16[8,500,500]{2,0,1:T(8,128)(2,1)S(1)}, bf16[8,500,500]{2,0,1:T(8,128)(2,1)}, u32[]{:S(2)}) %copy-start) | copy-done | bytes 4000024
  6.0 3.3 %copy.11.tail_ref = bf16[8,500,500]{2,1,0:T(8,128)(2,1)} copy(bf16[8,500,500]{2,0,1:T(8,128)(2,1)S(1)} %copy-done) | data formatting | bytes 8000000 | tf_op args[1]
  9.3 78.8 %shard_map.58 = (f32[1000,128]{1,0:T(8,128)}, f32[4000,128]{1,0:T(8,128)}, f32[4000,128]{1,0:T(8,128)}) custom-call(bf16[2,500,500]{2,1,0:T(8,128)(2,1)} %copy.10.head_ref, bf16[8,500,500]{2,1,0:T(8,128)(2,1)} %copy.11.tail_ref, bf16[500,1024]{1,0:T(8,128)(2,1)} %bitcast.6), custom_call_target="tpu_custom_call" | custom-call | tf_op jit(solution)/shard_map/pallas_call | solution.py:393
  88.2 1.9 %copy.16 = f32[1000,128]{1,0:T(8,128)} copy(f32[1000,128]{1,0:T(8,128)} %get-tuple-element.6) | data formatting | bytes 1024000
  90.0 0.0 copy-start.1
  90.0 3.1 %copy.17 = f32[4000,128]{1,0:T(8,128)} copy(f32[4000,128]{1,0:T(8,128)} %get-tuple-element.7) | data formatting | bytes 4096000
  93.2 0.0 copy-done.1
  93.2 1.3 %copy.18 = f32[4000,128]{1,0:T(8,128)} copy(f32[4000,128]{1,0:T(8,128)S(1)} %copy-done.1) | data formatting | bytes 4096000
Async XLA Ops:
  0.6 2.4 %copy-start.2 = (bf16[4000,128]{1,0:T(8,128)(2,1)S(1)}, bf16[4000,128]{1,0:T(8,128)(2,1)}, u32[]{:S(2)}) copy-start(bf16[4000,128]{1,0:T(8,128)(2,1)} %param.5) | copy-start | bytes 3072004
  3.5 2.5 %copy-start = (bf16[8,500,500]{2,0,1:T(8,128)(2,1)S(1)}, bf16[8,500,500]{2,0,1:T(8,128)(2,1)}, u32[]{:S(2)}) copy-start(bf16[8,500,500]{2,0,1:T(8,128)(2,1)} %param.4) | copy-start | bytes 12000004
  90.0 3.2 %copy-start.1 = (f32[4000,128]{1,0:T(8,128)S(1)}, f32[4000,128]{1,0:T(8,128)}, u32[]{:S(2)}) copy-start(f32[4000,128]{1,0:T(8,128)} %get-tuple-element.8) | copy-start | bytes 6144004

commit v3 on v2

--- a/solution.py
+++ b/solution.py
@@ -99,9 +99,10 @@
     return (sketch, back_now, back_next)
 
 
-def gathered_kernel(head_ref, tail_ref, probe_ref, sk_ref, now_ref, next_ref, m, px, st, acc, yacc,
+def gathered_kernel(head_ref, tail_ref, probe_ref, sk_ref, now_ref, next_ref, m, px, st, acc, yacc, head_in, tail_in, probe_in,
                     local_sem, zsend, ysend, ssend, piece_recv, sib_recv, xsend, xrecv):
     f32 = jnp.float32
+    order = acc.shape[1]
     r = lax.axis_index("row")
     c = lax.axis_index("col")
     other = 1 - c
@@ -109,10 +110,9 @@
     mate = r + 1 - 2 * y
     layers = lax.axis_size("row") // 2
 
-    load_head = pltpu.make_async_copy(head_ref, m.at[pl.ds(2 * r, 2)], local_sem.at[0])
-    load_probe = pltpu.make_async_copy(
-        probe_ref, px.at[:, pl.ds(pl.multiple_of((12 - 8 * c) * LANES, LANES), 8 * LANES)], local_sem.at[1])
-    load_tail = pltpu.make_async_copy(tail_ref, m.at[pl.ds(16 + 8 * c, 8)], local_sem.at[2])
+    load_head = pltpu.make_async_copy(head_ref, head_in, local_sem.at[0])
+    load_probe = pltpu.make_async_copy(probe_ref, probe_in, local_sem.at[1])
+    load_tail = pltpu.make_async_copy(tail_ref, tail_in, local_sem.at[2])
     load_head.start()
     load_probe.start()
     load_tail.start()
@@ -182,6 +182,8 @@
         return st.at[pl.ds(pl.multiple_of((12 - 8 * core) * LANES, LANES), 8 * LANES), :]
 
     load_head.wait()
+    for half in range(2):
+        m[2 * r + half] = head_in[:, half, :]
     along_y(r).start()
 
     @pl.when(z > 0)
@@ -193,8 +195,13 @@
         along_z(r, 1).start()
 
     load_probe.wait()
+    for j in range(8):
+        spot = pl.multiple_of((19 - 8 * c - j) * LANES, LANES)
+        px[:, pl.ds(spot, LANES)] = probe_in[j * order:(j + 1) * order, :]
     swap(probe_part, 0).start()
     load_tail.wait()
+    for j in range(8):
+        m[16 + 8 * c + j] = tail_in[:, j, :]
 
     @pl.when(c == 0)
     def _():
@@ -294,7 +301,6 @@
             st[pl.ds(spot, LANES), :] = flipped[half * LANES:(half + 1) * LANES]
     swap(sketch_part, 2).start()
     mine = (r // 4) == c
-    order = acc.shape[1]
 
     def row_copy():
         return pltpu.make_async_remote_copy(
@@ -385,8 +391,6 @@
 def gathered_body(markov_head, markov_tail, probes):
     order = markov_head.shape[1]
     columns = probes.shape[1]
-    blocks = probes.reshape(8, order, columns)[::-1]
-    wide = blocks.transpose(1, 0, 2).reshape(order, 8 * columns)
     anywhere = pl.BlockSpec(memory_space=pl.ANY)
     near = pl.BlockSpec(memory_space=pltpu.VMEM)
     dma = pltpu.SemaphoreType.DMA
@@ -403,11 +407,14 @@
             pltpu.VMEM((24 * columns, order), jnp.bfloat16),
             pltpu.VMEM((5, order, 2 * columns), jnp.float32),
             pltpu.VMEM((5 * columns, order), jnp.float32),
+            pltpu.VMEM((order, 2, order), jnp.bfloat16),
+            pltpu.VMEM((order, 8, order), jnp.bfloat16),
+            pltpu.VMEM((8 * order, columns), jnp.bfloat16),
             dma((3,)), dma((16,)), dma((8,)), dma((8,)), dma((8,)), dma((8,)), dma((4,)), dma((4,)),
         ],
         compiler_params=pltpu.CompilerParams(
             collective_id=0, has_side_effects=True, vmem_limit_bytes=56 * 1024 * 1024),
-    )(markov_head, markov_tail, wide)
+    )(markov_head.transpose(1, 0, 2), markov_tail.transpose(1, 0, 2), probes)
 
 
 def solution(mesh):

time: 94.7 us -> 88.1 us (0.930)
  local copies, waits for them, and re-layouts: 15 us -> 6.31 us
  Pallas kernels: 78.8 us -> 80.9 us
    unnamed x13 -> x5, local copies, waits for them, and re-layouts: 14.6 us -> 6.31 us
    pallas_call x1, Pallas kernels: 78.8 us -> 80.9 us  [gathered_body(): pl.pallas_call(gathered_kernel, out_shape=(jax.ShapeDtypeStruct((2 * orde...]
where the time goes in v3:
time: 88.1 us; the launch traced here: 87.9 us
  Pallas kernels  80.9 us (92%)
  local copies, waits for them, and re-layouts  6.31 us (7%)
    pallas_call x1, Pallas kernels, gathered_body(): pl.pallas_call(gathered_kernel, out_shape=(jax.ShapeDtypeStruct((2 * orde...  80.9 us
    unnamed x5, local copies, waits for them, and re-layouts  6.31 us

profile of v3, /device:TPU:1, one launch (start us, length us, event | category | flops | bytes accessed | tf_op | source)
XLA Modules:
  0.0 87.9 jit_solution(1118944305425554438)
XLA Ops:
  0.6 80.9 %shard_map.58 = (f32[1000,128]{1,0:T(8,128)}, f32[4000,128]{1,0:T(8,128)}, f32[4000,128]{1,0:T(8,128)}) custom-call(bf16[500,2,500]{2,1,0:T(2,128)(2,1)} %bitcast.3, bf16[500,8,500]{2,1,0:T(8,128)(2,1)} %bitcast.2, bf16[4000,128]{1,0:T(8,128)(2,1)} %probe_ref.1), custom_call_target="tpu_custom_call" | custom-call | tf_op jit(solution)/shard_map/pallas_call | solution.py:397
  81.6 1.9 %copy.9 = f32[1000,128]{1,0:T(8,128)} copy(f32[1000,128]{1,0:T(8,128)} %get-tuple-element.6) | data formatting | bytes 1024000
  83.4 0.0 copy-start
  83.4 3.1 %copy.10 = f32[4000,128]{1,0:T(8,128)} copy(f32[4000,128]{1,0:T(8,128)} %get-tuple-element.7) | data formatting | bytes 4096000
  86.6 0.0 copy-done
  86.6 1.3 %copy.11 = f32[4000,128]{1,0:T(8,128)} copy(f32[4000,128]{1,0:T(8,128)S(1)} %copy-done) | data formatting | bytes 4096000
Async XLA Ops:
  83.4 3.2 %copy-start = (f32[4000,128]{1,0:T(8,128)S(1)}, f32[4000,128]{1,0:T(8,128)}, u32[]{:S(2)}) copy-start(f32[4000,128]{1,0:T(8,128)} %get-tuple-element.8) | copy-start | bytes 6144004

commit v4 on v3

--- a/solution.py
+++ b/solution.py
@@ -142,24 +142,27 @@
     acc[...] = jnp.zeros_like(acc)
     pl.semaphore_wait(barrier, 2 + (z > 0).astype(jnp.int32) + (z < layers - 1).astype(jnp.int32))
 
-    def along_z(s, up):
-        return pltpu.make_async_remote_copy(
-            m.at[2 * s + c], m.at[2 * s + c], zsend.at[up * 8 + s], piece_recv.at[s],
+    def piece(k, h):
+        return m.at[k, pl.ds(256 * h, 256)]
+
+    def along_z(s, up, h):
+        return pltpu.make_async_remote_copy(
+            piece(2 * s + c, h), piece(2 * s + c, h), zsend.at[16 * up + 2 * s + h], piece_recv.at[2 * s + h],
             device_id={"row": r + 4 * up - 2, "col": c}, device_id_type=MESH)
 
-    def along_y(s):
-        return pltpu.make_async_remote_copy(
-            m.at[2 * s + c], m.at[2 * s + c], ysend.at[s], piece_recv.at[s],
+    def along_y(s, h):
+        return pltpu.make_async_remote_copy(
+            piece(2 * s + c, h), piece(2 * s + c, h), ysend.at[2 * s + h], piece_recv.at[2 * s + h],
             device_id={"row": mate, "col": c}, device_id_type=MESH)
 
-    def to_core(s):
-        return pltpu.make_async_remote_copy(
-            m.at[2 * s + c], m.at[2 * s + c], ssend.at[s], sib_recv.at[s],
+    def to_core(s, h):
+        return pltpu.make_async_remote_copy(
+            piece(2 * s + c, h), piece(2 * s + c, h), ssend.at[2 * s + h], sib_recv.at[2 * s + h],
             device_id={"row": r, "col": other}, device_id_type=MESH)
 
-    def from_core(s):
-        return pltpu.make_async_remote_copy(
-            m.at[2 * s + other], m.at[2 * s + other], ssend.at[s], sib_recv.at[s],
+    def from_core(s, h):
+        return pltpu.make_async_remote_copy(
+            piece(2 * s + other, h), piece(2 * s + other, h), ssend.at[2 * s + h], sib_recv.at[2 * s + h],
             device_id={"row": r, "col": other}, device_id_type=MESH)
 
     def swap(ref_of, slot):
@@ -183,16 +186,17 @@
 
     load_head.wait()
     for half in range(2):
-        m[2 * r + half] = head_in[:, half, :]
-    along_y(r).start()
-
-    @pl.when(z > 0)
-    def _():
-        along_z(r, 0).start()
-
-    @pl.when(z < layers - 1)
-    def _():
-        along_z(r, 1).start()
+        m[2 * r + half, 0:order] = head_in[:, half, :]
+    for h in (0, 1):
+        along_y(r, h).start()
+
+        @pl.when(z > 0)
+        def _(h=h):
+            along_z(r, 0, h).start()
+
+        @pl.when(z < layers - 1)
+        def _(h=h):
+            along_z(r, 1, h).start()
 
     load_probe.wait()
     for j in range(8):
@@ -201,7 +205,7 @@
     swap(probe_part, 0).start()
     load_tail.wait()
     for j in range(8):
-        m[16 + 8 * c + j] = tail_in[:, j, :]
+        m[16 + 8 * c + j, 0:order] = tail_in[:, j, :]
 
     @pl.when(c == 0)
     def _():
@@ -216,7 +220,7 @@
             @pl.when((lag >= 0) & (lag <= 16))
             def _():
                 spot = pl.multiple_of((19 - lag) * LANES, LANES)
-                acc[g] += jnp.dot(m[k], px[:, pl.ds(spot, 2 * LANES)], preferred_element_type=f32)
+                acc[g] += jnp.dot(m[k, 0:order], px[:, pl.ds(spot, 2 * LANES)], preferred_element_type=f32)
 
             return carry
 
@@ -228,7 +232,8 @@
     def use_chip(s):
         @pl.when(wanted(s, c))
         def _():
-            from_core(s).wait_recv()
+            from_core(s, 0).wait_recv()
+            from_core(s, 1).wait_recv()
             use(2 * s, 2)
 
     def each_side(base, distance, act):
@@ -240,58 +245,67 @@
             def _(s=s, up=up):
                 act(s, up)
 
-    def take_z(s, up):
-        along_y(s).wait_recv()
+    def take_z(s, up, h):
+        along_y(s, h).wait_recv()
         onward = (z < layers - 1) if up == 0 else (z > 0)
 
         @pl.when(onward)
         def _():
-            along_z(s, 1 - up).start()
-
-        along_y(s).start()
+            along_z(s, 1 - up, h).start()
+
+        along_y(s, h).start()
 
         @pl.when(wanted(s, other))
         def _():
-            to_core(s).start()
-
-    def take_y(s, up=0):
-        along_y(s).wait_recv()
+            to_core(s, h).start()
+
+    def take_y(s, h):
+        along_y(s, h).wait_recv()
 
         @pl.when(wanted(s, other))
         def _():
-            to_core(s).start()
+            to_core(s, h).start()
+
+    def arrive(distance, h):
+        each_side(r, distance, lambda s, up: take_z(s, up, h))
+        if distance == 1:
+            take_y(mate, h)
+        else:
+            each_side(mate, distance - 1, lambda s, up: take_y(s, h))
 
     swapped(probe_part, 0).wait_recv()
     use(16 + 8 * c, 7)
 
-    each_side(r, 1, take_z)
-    take_y(mate)
+    arrive(1, 0)
 
     @pl.when(wanted(r, c))
     def _():
         use(2 * r, 2)
+
+    arrive(1, 1)
 
     @pl.when(c == 1)
     def _():
         swapped(tail_part, 1).wait_recv()
         use(16, 4)
 
-    each_side(r, 2, take_z)
-    each_side(mate, 1, take_y)
+    arrive(2, 0)
 
     @pl.when(c == 1)
     def _():
         use(20, 4)
 
+    arrive(2, 1)
     use_chip(mate)
     each_side(r, 1, lambda s, up: use_chip(s))
-    each_side(r, 3, take_z)
-    each_side(mate, 2, take_y)
+    arrive(3, 0)
     each_side(r, 2, lambda s, up: use_chip(s))
+    arrive(3, 1)
     each_side(mate, 1, lambda s, up: use_chip(s))
-    each_side(mate, 3, take_y)
+    each_side(mate, 3, lambda s, up: take_y(s, 0))
     each_side(r, 3, lambda s, up: use_chip(s))
     each_side(mate, 2, lambda s, up: use_chip(s))
+    each_side(mate, 3, lambda s, up: take_y(s, 1))
     each_side(mate, 3, lambda s, up: use_chip(s))
 
     for g in range(4):
@@ -323,7 +337,7 @@
             for part in range(UNROLL[wide]):
                 lag = UNROLL[wide] * turn + part
                 spot = pl.multiple_of((19 - lag) * LANES, LANES)
-                term = jnp.dot(st[pl.ds(spot, rows), :], m[8 * c + first + lag], preferred_element_type=f32)
+                term = jnp.dot(st[pl.ds(spot, rows), :], m[8 * c + first + lag, 0:order], preferred_element_type=f32)
                 total = term if total is None else total + term
             yacc[0:rows] += total
             return carry
@@ -347,38 +361,36 @@
     def _():
         row_copy().wait_send()
 
-    def sent(s, up):
+    def sent(s, up, h):
         onward = (z < layers - 1) if up == 0 else (z > 0)
 
         @pl.when(onward)
         def _():
-            along_z(s, 1 - up).wait_send()
-
-        along_y(s).wait_send()
-
+            along_z(s, 1 - up, h).wait_send()
+
+        along_y(s, h).wait_send()
+        sent_core(s, h)
+
+    def sent_core(s, h):
         @pl.when(wanted(s, other))
         def _():
-            to_core(s).wait_send()
-
-    def sent_core(s, up=0):
-        @pl.when(wanted(s, other))
-        def _():
-            to_core(s).wait_send()
-
-    along_y(r).wait_send()
-
-    @pl.when(z > 0)
-    def _():
-        along_z(r, 0).wait_send()
-
-    @pl.when(z < layers - 1)
-    def _():
-        along_z(r, 1).wait_send()
-
-    sent_core(mate)
-    for distance in (1, 2, 3):
-        each_side(r, distance, sent)
-        each_side(mate, distance, sent_core)
+            to_core(s, h).wait_send()
+
+    for h in (0, 1):
+        along_y(r, h).wait_send()
+
+        @pl.when(z > 0)
+        def _(h=h):
+            along_z(r, 0, h).wait_send()
+
+        @pl.when(z < layers - 1)
+        def _(h=h):
+            along_z(r, 1, h).wait_send()
+
+        sent_core(mate, h)
+        for distance in (1, 2, 3):
+            each_side(r, distance, lambda s, up, h=h: sent(s, up, h))
+            each_side(mate, distance, lambda s, up, h=h: sent_core(s, h))
     swap(probe_part, 0).wait_send()
 
     @pl.when(c == 0)
@@ -402,7 +414,7 @@
         in_specs=[anywhere] * 3,
         out_specs=(near, near, near),
         scratch_shapes=[
-            pltpu.VMEM((32, order, order), jnp.bfloat16),
+            pltpu.VMEM((32, 512, order), jnp.bfloat16),
             pltpu.VMEM((order, 24 * columns), jnp.bfloat16),
             pltpu.VMEM((24 * columns, order), jnp.bfloat16),
             pltpu.VMEM((5, order, 2 * columns), jnp.float32),
@@ -410,7 +422,7 @@
             pltpu.VMEM((order, 2, order), jnp.bfloat16),
             pltpu.VMEM((order, 8, order), jnp.bfloat16),
             pltpu.VMEM((8 * order, columns), jnp.bfloat16),
-            dma((3,)), dma((16,)), dma((8,)), dma((8,)), dma((8,)), dma((8,)), dma((4,)), dma((4,)),
+            dma((3,)), dma((32,)), dma((16,)), dma((16,)), dma((16,)), dma((16,)), dma((4,)), dma((4,)),
         ],
         compiler_params=pltpu.CompilerParams(
             collective_id=0, has_side_effects=True, vmem_limit_bytes=56 * 1024 * 1024),

time: 88.1 us -> 84.5 us (0.959)
  the two profiles are of different devices: /device:TPU:1 before, /device:TPU:9 now
where the time goes in v4:
time: 84.5 us; the launch traced here: 84.3 us
  Pallas kernels  77.4 us (92%)
  local copies, waits for them, and re-layouts  6.31 us (7%)
    pallas_call x1, Pallas kernels, gathered_body(): pl.pallas_call(gathered_kernel, out_shape=(jax.ShapeDtypeStruct((2 * orde...  77.4 us
    unnamed x5, local copies, waits for them, and re-layouts  6.31 us

profile of v4, /device:TPU:9, one launch (start us, length us, event | category | flops | bytes accessed | tf_op | source)
XLA Modules:
  0.0 84.3 jit_solution(3183419272836232596)
XLA Ops:
  0.6 77.4 %shard_map.58 = (f32[1000,128]{1,0:T(8,128)}, f32[4000,128]{1,0:T(8,128)}, f32[4000,128]{1,0:T(8,128)}) custom-call(bf16[500,2,500]{2,1,0:T(2,128)(2,1)} %bitcast.3, bf16[500,8,500]{2,1,0:T(8,128)(2,1)} %bitcast.2, bf16[4000,128]{1,0:T(8,128)(2,1)} %probe_ref.1), custom_call_target="tpu_custom_call" | custom-call | tf_op jit(solution)/shard_map/pallas_call | solution.py:409
  78.0 1.9 %copy.9 = f32[1000,128]{1,0:T(8,128)} copy(f32[1000,128]{1,0:T(8,128)} %get-tuple-element.6) | data formatting | bytes 1024000
  79.9 0.0 copy-start
  79.9 3.1 %copy.10 = f32[4000,128]{1,0:T(8,128)} copy(f32[4000,128]{1,0:T(8,128)} %get-tuple-element.7) | data formatting | bytes 4096000
  83.0 0.0 copy-done
  83.0 1.3 %copy.11 = f32[4000,128]{1,0:T(8,128)} copy(f32[4000,128]{1,0:T(8,128)S(1)} %copy-done) | data formatting | bytes 4096000
Async XLA Ops:
  79.9 3.2 %copy-start = (f32[4000,128]{1,0:T(8,128)S(1)}, f32[4000,128]{1,0:T(8,128)}, u32[]{:S(2)}) copy-start(f32[4000,128]{1,0:T(8,128)} %get-tuple-element.8) | copy-start | bytes 6144004
